TPU v7x, 32 devices: a whole 2x2x4 slice. The times are simulated.
32 devices in a mesh: groups: 2 (over y), tensor: 8 (over z, x), seq: 2 (over core).
Axes of the slice: x: 2, y: 2, z: 4, core: 2. Of those that a mesh axis runs over, the one named last changes fastest.
Arguments:
- hidden_in: bfloat16 [4, 512, 2560], P(('groups', 'seq'), 'tensor'), parts along dimension 0, may hold values from -4 to 4
- span_order: int32 [4], P('groups'), parts along dimension 0, may hold values from 0 to 7, as said below
- norm_gain: float32 [2560], replicated, may hold values from 0.5 to 2
- w_query: bfloat16 [2560, 2048], P(None, 'tensor'), may hold values from -0.125 to 0.125
- w_keyval_t: bfloat16 [2048, 2560], P('tensor'), may hold values from -0.125 to 0.125
- q_gain: float32 [128], replicated, may hold values from 0.5 to 16
- k_gain: float32 [128], replicated, may hold values from 0.5 to 16
- w_out: bfloat16 [2048, 2560], P('tensor'), may hold values from -0.5 to 0.5
Outputs:
- hidden_out: bfloat16 [4, 512, 2560], P(('groups', 'seq'), 'tensor'), parts along dimension 0
There are 2 independent parts, one for each index of `groups`. A program takes and returns all parts, laid end to end along the dimension named above; an argument that names none is the same for every part. Nothing has to cross between parts.
Inputs may be any that keep to these rules, and one draw needn't show every extreme that they name: `span_order`: the 2 entries are different.
All inputs are finite; a program needn't handle non-finite values.
Results may differ from a plain program's by a relative error of at most 0.014.
The roundings to bfloat16 on the way count: a program that leaves them out, or rounds other values in their place, can miss the bound.
Values may be sent and summed in bfloat16 or wider, within the bound.
A program may use at most 64 MiB of HBM per device.

v0:
```python
import jax
import jax.numpy as jnp
from jax import lax
from jax.sharding import PartitionSpec as P

HD = 128
KV_HEADS = 8


epsilon = 1e-06


def normalize(vector, gain):
    vector = vector.astype(jnp.float32)
    return vector * lax.rsqrt(jnp.mean(vector * vector, axis=-1, keepdims=True) + epsilon) * gain


def rotate(vector, position):
    half_dim = vector.shape[-1] // 2
    inverse = 1000000.0 ** (-2.0 * jnp.arange(half_dim, dtype=jnp.float32) / vector.shape[-1])
    angles = position.astype(jnp.float32)[:, None] * inverse[None, :]
    cosine = jnp.cos(angles)
    sine = jnp.sin(angles)
    front = vector[:, :half_dim]
    back = vector[:, half_dim:]
    return jnp.concatenate([front * cosine - back * sine, back * cosine + front * sine], axis=-1)


def prepare_keys(key_rows, gain, position):
    blocks = rotate(normalize(key_rows, gain), position)
    return blocks.astype(jnp.bfloat16)


def body(hidden_in, span_order, norm_gain, w_query, w_keyval_t, q_gain, k_gain, w_out):
    own_rows = hidden_in[0]
    rows_here = own_rows.shape[0]
    tensor_size = lax.axis_size("tensor")
    seq_size = lax.axis_size("seq")
    span_len = rows_here * tensor_size
    heads_here = w_query.shape[1] // HD
    group_size = heads_here * tensor_size // KV_HEADS
    kv_count = max(1, heads_here // group_size)
    own_normed = normalize(own_rows, norm_gain).astype(jnp.bfloat16)
    gathered = lax.all_gather(own_normed, "tensor", axis=0, tiled=True)
    slot_index = lax.axis_index("seq")
    offsets = jnp.arange(span_len, dtype=jnp.int32)
    position = span_order[slot_index] * span_len + offsets
    key_pos = (span_order[:, None] * span_len + offsets[None, :]).reshape(seq_size * span_len)
    query_raw = jnp.dot(gathered, w_query, preferred_element_type=jnp.float32)
    kv_columns = lax.dot_general(
        w_keyval_t, gathered, (((1,), (1,)), ((), ())), preferred_element_type=jnp.float32
    ).astype(jnp.bfloat16)
    kv_first = lax.axis_index("tensor") * heads_here // group_size
    columns = lax.all_gather(kv_columns, "tensor", axis=0, tiled=True)
    key_t = lax.dynamic_slice_in_dim(columns, kv_first * HD, kv_count * HD, 0)
    value_t = lax.dynamic_slice_in_dim(columns, (KV_HEADS + kv_first) * HD, kv_count * HD, 0)
    own_keys = prepare_keys(key_t.T, k_gain, position)
    own_values = value_t.T
    all_keys, all_values = (
        lax.all_gather(own_keys, "seq", axis=0, tiled=True),
        lax.all_gather(own_values, "seq", axis=0, tiled=True),
    )
    visible = key_pos[None, :] <= position[:, None]
    pieces = []
    for local in range(heads_here):
        query_cols = query_raw[:, local * HD : (local + 1) * HD]
        queries = (rotate(normalize(query_cols, q_gain), position) * HD ** (-0.5)).astype(
            jnp.bfloat16
        )
        scores = lax.dot_general(
            queries, all_keys, (((1,), (1,)), ((), ())), preferred_element_type=jnp.float32
        )
        scores = jnp.where(visible, scores, -jnp.inf)
        largest = jnp.max(scores, axis=-1, keepdims=True)
        expos = jnp.exp(scores - largest)
        probs = (expos / jnp.sum(expos, axis=-1, keepdims=True)).astype(jnp.bfloat16)
        pieces.append(
            jnp.dot(probs, all_values, preferred_element_type=jnp.float32).astype(jnp.bfloat16)
        )
    attended = jnp.concatenate(pieces, axis=-1)
    summed = lax.psum_scatter(
        jnp.dot(attended, w_out, preferred_element_type=jnp.float32).astype(jnp.bfloat16),
        "tensor",
        scatter_dimension=0,
        tiled=True,
    ).astype(jnp.float32)
    return (own_rows.astype(jnp.float32) + summed).astype(jnp.bfloat16)[None]


def solution(mesh):
    placed = (
        P(("groups", "seq"), "tensor", None),
        P("groups"),
        P(),
        P(None, "tensor"),
        P("tensor", None),
        P(),
        P(),
        P("tensor", None),
    )
    return jax.shard_map(
        body,
        mesh=mesh,
        in_specs=placed,
        out_specs=P(("groups", "seq"), "tensor", None),
        check_vma=False,
    )
```

profile of v0, /device:TPU:0, one launch (start us, length us, event | category | flops | bytes accessed | tf_op | source)
XLA Modules:
  0.0 209.4 jit_solution(4205084987232322128)
XLA Ops:
  6.5 1.2 fusion.3
  7.8 1.9 fusion.5
  9.6 0.0 all-gather.3.cloned.1.call-update
  9.7 0.0 copy-start.4
  9.7 0.0 all-gather.5.cloned.1.call-start
  9.7 57.4 %all-gather.3.cloned.1.call-done = bf16[512,2560]{1,0:T(8,128)(2,1)} async-done(((bf16[64,2560]{1,0:T(8,128)(2,1)}), bf16[512,2560]{1,0:T(8,128)(2,1)}) %all-gather.3.cloned.1.call-update) | async-done | bytes 2621456 | tf_op jit(solution)/shard_map/all_gather | solution.py:44
  67.2 3.7 %fusion.2 = bf16[256,512]{1,0:T(8,128)(2,1)} fusion(bf16[512,2560]{1,0:T(8,128)(2,1)} %all-gather.3.cloned.1.call-done, bf16[256,2560]{1,0:T(8,128)(2,1)} %param.12), kind=kOutput, calls=%fused_computation.10 | convolution fusion | flops 671219712 | bytes 4194304 | tf_op jit(solution)/shard_map/dot_general | solution.py:50
  70.9 0.0 all-gather.5.cloned.1.call-update
  70.9 0.0 reduce-scatter.2.cloned.1.call-start
  71.0 0.6 dynamic_slice.9
  71.5 0.1 add_bitcast_fusion
  72.2 0.0 copy-start.2
  72.2 2.6 %fusion.48 = f32[512,256]{0,1:T(8,128)S(1)} fusion(bf16[512,2560]{1,0:T(8,128)(2,1)} %all-gather.3.cloned.1.call-done, bf16[2560,256]{1,0:T(8,128)(2,1)S(1)} %copy-done.4), kind=kOutput, calls=%fused_computation.79 | convolution fusion | flops 671088640 | bytes 4456448 | tf_op jit(solution)/shard_map/dot_general | solution.py:49
  74.9 0.1 multiply_reduce_fusion.1
  75.0 0.1 multiply_multiply_fusion.1
  75.1 43.8 %all-gather.5.cloned.1.call-done = bf16[2048,512]{1,0:T(8,128)(2,1)} async-done(((bf16[256,512]{1,0:T(8,128)(2,1)}), bf16[2048,512]{1,0:T(8,128)(2,1)}) %all-gather.5.cloned.1.call-update) | async-done | bytes 2097168 | tf_op jit(solution)/shard_map/all_gather | solution.py:54
  118.9 1.0 fusion.8
  119.9 0.9 dynamic-slice_bitcast_fusion
  120.8 2.0 all_gather.15
  122.8 1.0 fusion.10
  123.8 0.6 fusion.28
  124.4 2.0 all_gather.14
  126.4 0.6 fusion.46
  127.0 0.5 fusion.1
  127.5 0.5 convolution_convert_fusion.2
  128.0 0.6 fusion.47
  128.6 0.5 fusion
  129.1 0.5 convolution_convert_fusion.3
  129.7 2.4 %convolution_convert_fusion = bf16[512,2560]{1,0:T(8,128)(2,1)} fusion(bf16[256,2560]{1,0:T(8,128)(2,1)S(1)} %copy-done, bf16[512,128]{1,0:T(8,128)(2,1)S(1)} %convolution_convert_fusion.2, bf16[512,128]{1,0:T(8,128)(2,1)S(1)} %convolution_convert_fusion.3), kind=kOutput, calls=%fused_computation | convolution fusion | flops 672923648 | bytes 4194304 | tf_op jit(solution)/shard_map/dot_general | solution.py:82
  132.0 0.0 reduce-scatter.2.cloned.1.call-update
  132.1 69.1 %reduce-scatter.2.cloned.1.call-done = bf16[64,2560]{1,0:T(8,128)(2,1)} async-done(((bf16[512,2560]{1,0:T(8,128)(2,1)}), bf16[64,2560]{1,0:T(8,128)(2,1)}) %reduce-scatter.2.cloned.1.call-update) | async-done | bytes 327696 | tf_op jit(solution)/shard_map/reduce_scatter | solution.py:81
  201.1 1.8 fusion.7
  (20 shorter events, 0.1 us)
Async XLA Ops:
  6.5 123.1 %copy-start = (bf16[256,2560]{1,0:T(8,128)(2,1)S(1)}, bf16[256,2560]{1,0:T(8,128)(2,1)}, u32[]{:S(2)}) copy-start(bf16[256,2560]{1,0:T(8,128)(2,1)} %param.15) | copy-start | bytes 3932164
  6.5 60.6 %all-gather.3.cloned.1.call-start = ((), (), s32[]{:S(2)}) async-start(), calls=%async_computation.1 | async-start | bytes 2949120 | tf_op jit(solution)/shard_map/all_gather | solution.py:44
  9.7 61.3 %copy-start.5 = (s32[2]{0:T(128)S(1)}, s32[2]{0:T(128)}, u32[]{:S(2)}) copy-start(s32[2]{0:T(128)} %param.9) | copy-start | bytes 28
  9.7 62.5 %copy-start.4 = (bf16[2560,256]{1,0:T(8,128)(2,1)S(1)}, bf16[2560,256]{1,0:T(8,128)(2,1)}, u32[]{:S(2)}) copy-start(bf16[2560,256]{1,0:T(8,128)(2,1)} %param.11) | copy-start | bytes 3932164
  9.7 109.2 %all-gather.5.cloned.1.call-start = ((), (), s32[]{:S(2)}) async-start(), calls=%async_computation.2 | async-start | bytes 2359296 | tf_op jit(solution)/shard_map/all_gather | solution.py:54
  70.9 130.3 %reduce-scatter.2.cloned.1.call-start = ((), (), s32[]{:S(2)}) async-start(), calls=%async_computation.3 | async-start | bytes 2949120 | tf_op jit(solution)/shard_map/reduce_scatter | solution.py:81
  72.2 2.7 %copy-start.2 = (f32[128]{0:T(128)S(1)}, f32[128]{0:T(128)}, u32[]{:S(2)}) copy-start(f32[128]{0:T(128)} %param.13) | copy-start | bytes 1540
  74.9 47.9 %copy-start.3 = (f32[128]{0:T(128)S(1)}, f32[128]{0:T(128)}, u32[]{:S(2)}) copy-start(f32[128]{0:T(128)} %param.14) | copy-start | bytes 1540
  132.0 69.1 %copy-start.1 = (bf16[1,64,2560]{2,1,0:T(8,128)(2,1)S(1)}, bf16[1,64,2560]{2,1,0:T(8,128)(2,1)}, u32[]{:S(2)}) copy-start(bf16[1,64,2560]{2,1,0:T(8,128)(2,1)} %param.8) | copy-start | bytes 983044
Sparse Core Ops, SparseCore 0:
  9.8 57.3 all-gather.2
  71.0 47.8 all-gather.4
  132.2 68.9 reduce-scatter.1
where the time goes:
time: 210 us; the launch traced here: 209 us
  waiting for transfers between devices  170 us (81%)
  between operations  13.8 us (7%)
  matrix products  10.9 us (5%)
  other arithmetic  8.75 us (4%)
  blocking collectives  3.99 us (2%)
    reduce_scatter x1, waiting for transfers between devices, body(): lax.psum_scatter(jnp.dot(attended, w_out, preferred_element_type=jnp.floa...  69.1 us
    all_gather x1, waiting for transfers between devices, body(): gathered = lax.all_gather(own_normed, 'tensor', axis=0, tiled=True)  57.4 us
    all_gather x1, waiting for transfers between devices, body(): columns = lax.all_gather(kv_columns, 'tensor', axis=0, tiled=True)  43.8 us
  transfers between devices with their start and end apart: 3, of which 3 were waited for; matrix products, arithmetic and copies ran while one was open for 2% of the time, Pallas kernels for 0%

commit v1 on v0

--- a/solution.py
+++ b/solution.py
@@ -1,6 +1,9 @@
 import jax
 import jax.numpy as jnp
+import numpy as np
 from jax import lax
+from jax.experimental import pallas as pl
+from jax.experimental.pallas import tpu as pltpu
 from jax.sharding import PartitionSpec as P
 
 HD = 128
@@ -87,6 +90,376 @@
     return (own_rows.astype(jnp.float32) + summed).astype(jnp.bfloat16)[None]
 
 
+MESH = pl.DeviceIdType.MESH
+Z = 4
+X = 2
+
+
+def layer_kernel(
+    span_ref, hidden_ref, gain_ref, inverse_ref, q_gain_ref, k_gain_ref, wq_hbm, wkv_hbm, wo_hbm,
+    out_ref,
+    rows_ref, wq_ref, wkv_ref, wo_ref, cos_ref, sin_ref, query_ref, kv_send, kv_in, key_own, key_other,
+    value_other, part_ref, x_in, up_in, down_in, line_out,
+    w_sem, row_recv, row_x_send, row_line_send, row_line_send2, kv_ssem, kv_rsem, pair_ssem, pair_rsem,
+    x_ssem, x_rsem, line_ssem, up_rsem, down_rsem,
+):
+    t = lax.axis_index("tensor")
+    s = lax.axis_index("seq")
+    z = t // X
+    x = t % X
+    block = hidden_ref.shape[0]
+    chunk = X * block
+    span_len = Z * chunk
+    x_peer = z * X + (1 - x)
+    low = z // 2
+    far = z * low + (1 - low) * (3 - z)
+    near = [far, 5 - far, 1, 0]
+    order = [low * v + (1 - low) * (3 - v) for v in near]
+
+    weight_copies = [
+        pltpu.make_async_copy(wq_hbm, wq_ref, w_sem.at[0]),
+        pltpu.make_async_copy(wkv_hbm, wkv_ref, w_sem.at[1]),
+        pltpu.make_async_copy(wo_hbm, wo_ref, w_sem.at[2]),
+    ]
+    for copy in weight_copies:
+        copy.start()
+
+    barrier = pltpu.get_barrier_semaphore()
+    for step in range(1, Z * X):
+        pl.semaphore_signal(
+            barrier, inc=1, device_id={"tensor": (t + step) % (Z * X)}, device_id_type=MESH
+        )
+    pl.semaphore_signal(barrier, inc=1, device_id={"seq": 1 - s}, device_id_type=MESH)
+
+    own = hidden_ref[...].astype(jnp.float32)
+    scale = lax.rsqrt(jnp.mean(own * own, axis=-1, keepdims=True) + epsilon)
+    own_start = pl.multiple_of(t * block, block)
+    rows_ref[pl.ds(own_start, block), :] = (own * scale * gain_ref[...]).astype(jnp.bfloat16)
+    pl.semaphore_wait(barrier, Z * X)
+
+    def row_copy(zb, xb, target, send_sem):
+        place = pl.ds(pl.multiple_of((zb * X + xb) * block, block), block)
+        return pltpu.make_async_remote_copy(
+            src_ref=rows_ref.at[place, :],
+            dst_ref=rows_ref.at[place, :],
+            send_sem=send_sem.at[zb],
+            recv_sem=row_recv.at[zb * X + xb],
+            device_id={"tensor": target},
+            device_id_type=MESH,
+        )
+
+    def line_up(zb):
+        return row_copy(zb, x, (t + X) % (Z * X), row_line_send)
+
+    def line_down(zb):
+        return row_copy(zb, x, (t + Z * X - X) % (Z * X), row_line_send2)
+
+    def across(zb):
+        return row_copy(zb, x, x_peer, row_x_send)
+
+    def forward(zb):
+        @pl.when((zb <= z) & (z < Z - 1))
+        def _():
+            line_up(zb).start()
+
+        @pl.when((zb >= z) & (z > 0))
+        def _():
+            line_down(zb).start()
+
+        across(zb).start()
+
+    forward(z)
+
+    inverse = inverse_ref[...]
+    position = span_ref[s] * span_len + lax.broadcasted_iota(jnp.int32, (span_len, HD), 0)
+    angles = position.astype(jnp.float32) * inverse
+    cos_ref[...] = jnp.cos(angles)
+    lane = lax.broadcasted_iota(jnp.int32, (span_len, HD), 1)
+    sine = jnp.sin(angles)
+    sin_ref[...] = jnp.where(lane < HD // 2, -sine, sine)
+
+    def norm_rotate(v, gain, zb):
+        place = pl.ds(pl.multiple_of(zb * chunk, chunk), chunk)
+        v = v * lax.rsqrt(jnp.mean(v * v, axis=-1, keepdims=True) + epsilon) * gain
+        return v * cos_ref[place, :] + pltpu.roll(v, HD // 2, 1) * sin_ref[place, :]
+
+    kind = t // Z
+
+    def kv_copy(zb, j):
+        return pltpu.make_async_remote_copy(
+            src_ref=kv_send.at[zb, j],
+            dst_ref=kv_in.at[kind, pl.ds(pl.multiple_of(zb * chunk, chunk), chunk), :],
+            send_sem=kv_ssem.at[zb, j],
+            recv_sem=kv_rsem.at[kind, zb],
+            device_id={"tensor": (2 * t + j) % (Z * X)},
+            device_id_type=MESH,
+        )
+
+    def project(zb):
+        place = pl.ds(pl.multiple_of(zb * chunk, chunk), chunk)
+        rows = rows_ref[place, :]
+        kv = lax.dot_general(
+            rows, wkv_ref[...], (((1,), (1,)), ((), ())), preferred_element_type=jnp.float32
+        ).astype(jnp.bfloat16)
+        for j in range(2):
+            kv_send[zb, j] = kv[:, j * HD : (j + 1) * HD]
+            here = (2 * t + j) % (Z * X) == t
+
+            @pl.when(here)
+            def _():
+                kv_in[kind, place, :] = kv_send[zb, j]
+
+            @pl.when(jnp.logical_not(here))
+            def _():
+                kv_copy(zb, j).start()
+
+        raw = jnp.dot(rows, wq_ref[...], preferred_element_type=jnp.float32)
+        for j in range(2):
+            q = norm_rotate(raw[:, j * HD : (j + 1) * HD], q_gain_ref[...], zb) * HD ** (-0.5)
+            query_ref[zb, j * chunk : (j + 1) * chunk, :] = q.astype(jnp.bfloat16)
+
+    weight_copies[1].wait()
+    weight_copies[0].wait()
+    for k in range(1, Z):
+        zb = order[k]
+        row_copy(zb, x, x_peer, row_x_send).wait_recv()
+        forward(zb)
+        row_copy(order[k - 1], 1 - x, x_peer, row_x_send).wait_recv()
+        project(order[k - 1])
+    row_copy(order[Z - 1], 1 - x, x_peer, row_x_send).wait_recv()
+    project(order[Z - 1])
+
+    def pair_copy(index, zb, source, target):
+        place = pl.ds(zb * chunk, chunk)
+        return pltpu.make_async_remote_copy(
+            src_ref=source.at[place, :],
+            dst_ref=target.at[place, :],
+            send_sem=pair_ssem.at[index, zb],
+            recv_sem=pair_rsem.at[index, zb],
+            device_id={"seq": 1 - s},
+            device_id_type=MESH,
+        )
+
+    def kv_arrived(which, zb):
+        @pl.when((t // 2 + which * Z) != t)
+        def _():
+            pltpu.make_async_remote_copy(
+                src_ref=kv_send.at[zb, 0],
+                dst_ref=kv_in.at[which, pl.ds(zb * chunk, chunk), :],
+                send_sem=kv_ssem.at[zb, 0],
+                recv_sem=kv_rsem.at[which, zb],
+                device_id={"tensor": x_peer},
+                device_id_type=MESH,
+            ).wait_recv()
+
+    values = kv_in.at[1]
+    for zb in range(Z):
+        kv_arrived(0, zb)
+        place = slice(zb * chunk, (zb + 1) * chunk)
+        raw = kv_in[0, place, :].astype(jnp.float32)
+        key_own[place, :] = norm_rotate(raw, k_gain_ref[...], zb).astype(jnp.bfloat16)
+        pair_copy(0, zb, key_own, key_other).start()
+        kv_arrived(1, zb)
+        pair_copy(1, zb, values, value_other).start()
+    weight_copies[2].wait()
+    for zb in range(Z):
+        pair_copy(0, zb, key_own, key_other).wait_recv()
+        pair_copy(1, zb, values, value_other).wait_recv()
+
+    hide = jnp.where(span_ref[1 - s] < span_ref[s], 0.0, -1e30).astype(jnp.float32)
+
+    def attend(zb):
+        q = query_ref[zb]
+        nt = (((1,), (1,)), ((), ()))
+        mine = lax.dot_general(q, key_own[...], nt, preferred_element_type=jnp.float32)
+        others = lax.dot_general(q, key_other[...], nt, preferred_element_type=jnp.float32) + hide
+        row = lax.broadcasted_iota(jnp.int32, mine.shape, 0) % chunk + zb * chunk
+        column = lax.broadcasted_iota(jnp.int32, mine.shape, 1)
+        mine = jnp.where(column <= row, mine, -jnp.inf)
+        largest = jnp.maximum(
+            jnp.max(mine, axis=-1, keepdims=True), jnp.max(others, axis=-1, keepdims=True)
+        )
+        mine = jnp.exp(mine - largest)
+        others = jnp.exp(others - largest)
+        total = jnp.sum(mine, axis=-1, keepdims=True) + jnp.sum(others, axis=-1, keepdims=True)
+        share = 1.0 / total
+        result = jnp.dot(
+            (mine * share).astype(jnp.bfloat16), kv_in[1], preferred_element_type=jnp.float32
+        ) + jnp.dot(
+            (others * share).astype(jnp.bfloat16), value_other[...], preferred_element_type=jnp.float32
+        )
+        result = result.astype(jnp.bfloat16)
+        joined = jnp.concatenate([result[:chunk], result[chunk:]], axis=-1)
+        part_ref[zb] = jnp.dot(joined, wo_ref[...], preferred_element_type=jnp.float32).astype(
+            jnp.bfloat16
+        )
+
+    def part_copy(zb):
+        place = pl.ds(pl.multiple_of((1 - x) * block, block), block)
+        return pltpu.make_async_remote_copy(
+            src_ref=part_ref.at[zb, place, :],
+            dst_ref=x_in.at[zb],
+            send_sem=x_ssem.at[zb],
+            recv_sem=x_rsem.at[zb],
+            device_id={"tensor": x_peer},
+            device_id_type=MESH,
+        )
+
+    def sum_up(zb):
+        return pltpu.make_async_remote_copy(
+            src_ref=line_out.at[zb], dst_ref=up_in.at[zb], send_sem=line_ssem.at[zb],
+            recv_sem=up_rsem.at[zb], device_id={"tensor": (t + X) % (Z * X)}, device_id_type=MESH,
+        )
+
+    def sum_down(zb):
+        return pltpu.make_async_remote_copy(
+            src_ref=line_out.at[zb], dst_ref=down_in.at[zb], send_sem=line_ssem.at[zb],
+            recv_sem=down_rsem.at[zb], device_id={"tensor": (t + Z * X - X) % (Z * X)},
+            device_id_type=MESH,
+        )
+
+    back = order[::-1]
+    for zb in back:
+        attend(zb)
+        part_copy(zb).start()
+
+    own_half = pl.ds(pl.multiple_of(x * block, block), block)
+
+    def pair_sum(zb):
+        return part_ref[zb, own_half, :].astype(jnp.float32) + x_in[zb].astype(jnp.float32)
+
+    for zb in back[: Z - 1]:
+        part_copy(zb).wait_recv()
+
+        @pl.when(zb > z)
+        def _():
+            @pl.when(z > 0)
+            def _():
+                sum_up(zb).wait_recv()
+                line_out[zb] = (pair_sum(zb) + up_in[zb].astype(jnp.float32)).astype(jnp.bfloat16)
+
+            @pl.when(z == 0)
+            def _():
+                line_out[zb] = pair_sum(zb).astype(jnp.bfloat16)
+
+            sum_up(zb).start()
+
+        @pl.when(zb < z)
+        def _():
+            @pl.when(z < Z - 1)
+            def _():
+                sum_down(zb).wait_recv()
+                line_out[zb] = (pair_sum(zb) + down_in[zb].astype(jnp.float32)).astype(jnp.bfloat16)
+
+            @pl.when(z == Z - 1)
+            def _():
+                line_out[zb] = pair_sum(zb).astype(jnp.bfloat16)
+
+            sum_down(zb).start()
+
+    part_copy(z).wait_recv()
+    total = hidden_ref[...].astype(jnp.float32) + pair_sum(z)
+
+    @pl.when(z == 0)
+    def _():
+        sum_down(z).wait_recv()
+        out_ref[...] = (total + down_in[z].astype(jnp.float32)).astype(jnp.bfloat16)
+
+    @pl.when(z == Z - 1)
+    def _():
+        sum_up(z).wait_recv()
+        out_ref[...] = (total + up_in[z].astype(jnp.float32)).astype(jnp.bfloat16)
+
+    @pl.when((z > 0) & (z < Z - 1))
+    def _():
+        sum_down(z).wait_recv()
+        sum_up(z).wait_recv()
+        out_ref[...] = (
+            total + down_in[z].astype(jnp.float32) + up_in[z].astype(jnp.float32)
+        ).astype(jnp.bfloat16)
+
+    for zb in range(Z):
+        across(zb).wait_send()
+        part_copy(zb).wait_send()
+        pair_copy(0, zb, key_own, key_other).wait_send()
+        pair_copy(1, zb, values, value_other).wait_send()
+
+        @pl.when((zb <= z) & (z < Z - 1))
+        def _():
+            line_up(zb).wait_send()
+
+        @pl.when((zb >= z) & (z > 0))
+        def _():
+            line_down(zb).wait_send()
+
+        @pl.when(zb != z)
+        def _():
+            sum_up(zb).wait_send()
+
+        for j in range(2):
+            @pl.when((2 * t + j) % (Z * X) != t)
+            def _():
+                kv_copy(zb, j).wait_send()
+
+
+def fused_body(hidden_in, span_order, norm_gain, w_query, w_keyval_t, q_gain, k_gain, w_out):
+    _, block, width = hidden_in.shape
+    chunk = X * block
+    span_len = Z * chunk
+    inverse = 1000000.0 ** (-2.0 * np.arange(HD // 2) / HD)
+    inverse = jnp.asarray(np.concatenate([inverse, inverse])[None], jnp.float32)
+    vmem = pl.BlockSpec(memory_space=pltpu.VMEM)
+    anywhere = pl.BlockSpec(memory_space=pl.ANY)
+    bf16 = jnp.bfloat16
+    dma = pltpu.SemaphoreType.DMA
+    out = pl.pallas_call(
+        layer_kernel,
+        out_shape=jax.ShapeDtypeStruct((block, width), bf16),
+        in_specs=[pl.BlockSpec(memory_space=pltpu.SMEM)] + [vmem] * 5 + [anywhere] * 3,
+        out_specs=vmem,
+        scratch_shapes=[
+            pltpu.VMEM((span_len, width), bf16),
+            pltpu.VMEM(w_query.shape, bf16),
+            pltpu.VMEM(w_keyval_t.shape, bf16),
+            pltpu.VMEM(w_out.shape, bf16),
+            pltpu.VMEM((span_len, HD), jnp.float32),
+            pltpu.VMEM((span_len, HD), jnp.float32),
+            pltpu.VMEM((Z, 2 * chunk, HD), bf16),
+            pltpu.VMEM((Z, 2, chunk, HD), bf16),
+            pltpu.VMEM((2, span_len, HD), bf16),
+            pltpu.VMEM((span_len, HD), bf16),
+            pltpu.VMEM((span_len, HD), bf16),
+            pltpu.VMEM((span_len, HD), bf16),
+            pltpu.VMEM((Z, chunk, width), bf16),
+            pltpu.VMEM((Z, block, width), bf16),
+            pltpu.VMEM((Z, block, width), bf16),
+            pltpu.VMEM((Z, block, width), bf16),
+            pltpu.VMEM((Z, block, width), bf16),
+            dma((3,)),
+            dma((Z * X,)),
+            dma((Z,)),
+            dma((Z,)),
+            dma((Z,)),
+            dma((Z, 2)),
+            dma((2, Z)),
+            dma((2, Z)),
+            dma((2, Z)),
+            dma((Z,)),
+            dma((Z,)),
+            dma((Z,)),
+            dma((Z,)),
+            dma((Z,)),
+        ],
+        compiler_params=pltpu.CompilerParams(
+            collective_id=0, has_side_effects=True, vmem_limit_bytes=48 * 1024 * 1024
+        ),
+    )(
+        span_order, hidden_in[0], norm_gain[None], inverse, q_gain[None], k_gain[None],
+        w_query, w_keyval_t, w_out,
+    )
+    return out[None]
+
+
 def solution(mesh):
     placed = (
         P(("groups", "seq"), "tensor", None),
@@ -98,8 +471,18 @@
         P(),
         P("tensor", None),
     )
+    def chosen(hidden_in, span_order, norm_gain, w_query, *rest):
+        fits = (
+            mesh.shape["tensor"] == Z * X
+            and mesh.shape["seq"] == 2
+            and w_query.shape[1] == 2 * HD
+            and hidden_in.shape[1] % 16 == 0
+        )
+        run = fused_body if fits else body
+        return run(hidden_in, span_order, norm_gain, w_query, *rest)
+
     return jax.shard_map(
-        body,
+        chosen,
         mesh=mesh,
         in_specs=placed,
         out_specs=P(("groups", "seq"), "tensor", None),

time: 210 us -> 93 us (0.44)
  waiting for transfers between devices: 170 us -> 0 us
  Pallas kernels: 0 us -> 83.7 us
  between operations: 13.8 us -> 0.02 us
  matrix products: 10.9 us -> 0 us
  other arithmetic: 8.75 us -> 0 us
  local copies, waits for them, and re-layouts: 1.51 us -> 8.98 us
  blocking collectives: 3.99 us -> 0 us
    all_gather x2 -> x0, waiting for transfers between devices: 101 us -> none  [the longest x1 57.4 us: body(): gathered = lax.all_gather(own_normed, 'tensor', axis=0, tiled=True)]
    pallas_call x0 -> x1, Pallas kernels: none -> 83.7 us  [fused_body(): pl.pallas_call(layer_kernel, out_shape=jax.ShapeDtypeStruct((block, width...]
    reduce_scatter x1 -> x0, waiting for transfers between devices: 69.1 us -> none  [body(): lax.psum_scatter(jnp.dot(attended, w_out, preferred_element_type=jnp.floa...]
    dot_general x7 -> x0, matrix products: 10.9 us -> none  [the longest x1 3.68 us: body(): lax.dot_general(w_keyval_t, gathered, (((1,), (1,)), ((), ())), preferred...]
    unnamed x13 -> x17, local copies, waits for them, and re-layouts: 0.04 us -> 8.26 us
    all_gather x2 -> x0, blocking collectives: 3.99 us -> none  [the longest x1 1.99 us: body(): lax.all_gather(own_values, 'seq', axis=0, tiled=True)]
    reduce_sum x5 -> x0, other arithmetic: 3.28 us -> none  [the longest x3 2.25 us: normalize(): jnp.mean(vector * vector, axis=-1, keepdims=True) + epsilon]
  transfers between devices with their start and end apart: 3 -> 0, of which waited for: 3 -> 0; matrix products, arithmetic and copies ran while one was open for 2% -> 0% of each run, Pallas kernels for 0% -> 0%
where the time goes in v1:
time: 93 us; the launch traced here: 92.7 us
  Pallas kernels  83.7 us (90%)
  local copies, waits for them, and re-layouts  8.98 us (10%)
    pallas_call x1, Pallas kernels, fused_body(): pl.pallas_call(layer_kernel, out_shape=jax.ShapeDtypeStruct((block, width...  83.7 us
    unnamed x17, local copies, waits for them, and re-layouts  8.26 us

profile of v1, /device:TPU:0, one launch (start us, length us, event | category | flops | bytes accessed | tf_op | source)
XLA Modules:
  0.0 92.7 jit_solution(15619448639459519856)
XLA Ops:
  0.0 0.7 broadcast_in_dim.12.gain_ref
  0.7 0.0 copy-start
  0.7 1.3 %copy-done = bf16[2560,256]{1,0:T(8,128)(2,1)S(1)} copy-done((bf16[2560,256]{1,0:T(8,128)(2,1)S(1)}, bf16[2560,256]{1,0:T(8,128)(2,1)}, u32[]{:S(2)}) %copy-start) | copy-done | bytes 1310744
  2.0 0.0 copy-start.1
  2.0 1.3 %copy-done.1 = bf16[256,2560]{1,0:T(8,128)(2,1)S(1)} copy-done((bf16[256,2560]{1,0:T(8,128)(2,1)S(1)}, bf16[256,2560]{1,0:T(8,128)(2,1)}, u32[]{:S(2)}) %copy-start.1) | copy-done | bytes 1310744
  3.3 0.0 copy-start.2
  3.4 1.3 %copy-done.2 = bf16[256,2560]{1,0:T(8,128)(2,1)S(1)} copy-done((bf16[256,2560]{1,0:T(8,128)(2,1)S(1)}, bf16[256,2560]{1,0:T(8,128)(2,1)}, u32[]{:S(2)}) %copy-start.2) | copy-done | bytes 1310744
  4.7 0.0 copy-start.3
  4.7 1.0 %copy-done.3 = bf16[1,64,2560]{2,1,0:T(8,128)(2,1)S(1)} copy-done((bf16[1,64,2560]{2,1,0:T(8,128)(2,1)S(1)}, bf16[1,64,2560]{2,1,0:T(8,128)(2,1)}, u32[]{:S(2)}) %copy-start.3) | copy-done | bytes 327704
  5.6 0.0 copy-start.4
  5.6 0.7 copy-done.4
  6.3 0.0 copy-start.5
  6.3 0.7 copy-done.5
  7.0 0.0 copy-start.6
  7.0 0.7 copy-done.6
  7.6 0.0 copy-start.7
  7.6 0.7 copy-done.7
  8.3 83.7 %shard_map.91 = bf16[64,2560]{1,0:T(8,128)(2,1)S(1)} custom-call(s32[2]{0:T(128)S(1)} %copy-done.4, bf16[64,2560]{1,0:T(8,128)(2,1)S(1)} %bitcast.5, f32[1,2560]{1,0:T(1,128)S(1)} %broadcast_in_dim.12.gain_ref, f32[1,128]{1,0:T(1,128)S(1)} %copy-done.7, f32[1,128]{1,0:T(1,128)S(1)} %bitcast.6, f32[1,128]{1,0:T(1,128)S(1)} %bitcast.7, ...), custom_call_target="tpu_custom_call" | custom-call | tf_op jit(solution)/shard_map/pallas_call | solution.py:415
  92.0 0.7 copy.11
Async XLA Ops:
  0.7 1.3 %copy-start = (bf16[2560,256]{1,0:T(8,128)(2,1)S(1)}, bf16[2560,256]{1,0:T(8,128)(2,1)}, u32[]{:S(2)}) copy-start(bf16[2560,256]{1,0:T(8,128)(2,1)} %wq_hbm.1) | copy-start | bytes 3932164
  2.0 1.3 %copy-start.1 = (bf16[256,2560]{1,0:T(8,128)(2,1)S(1)}, bf16[256,2560]{1,0:T(8,128)(2,1)}, u32[]{:S(2)}) copy-start(bf16[256,2560]{1,0:T(8,128)(2,1)} %wkv_hbm.1) | copy-start | bytes 3932164
  3.3 1.3 %copy-start.2 = (bf16[256,2560]{1,0:T(8,128)(2,1)S(1)}, bf16[256,2560]{1,0:T(8,128)(2,1)}, u32[]{:S(2)}) copy-start(bf16[256,2560]{1,0:T(8,128)(2,1)} %wo_hbm.1) | copy-start | bytes 3932164
  4.7 1.0 %copy-start.3 = (bf16[1,64,2560]{2,1,0:T(8,128)(2,1)S(1)}, bf16[1,64,2560]{2,1,0:T(8,128)(2,1)}, u32[]{:S(2)}) copy-start(bf16[1,64,2560]{2,1,0:T(8,128)(2,1)} %param.9) | copy-start | bytes 983044
  5.6 0.7 copy-start.4
  6.3 0.7 copy-start.5
  7.0 0.7 copy-start.6
  7.6 0.7 copy-start.7

commit v2 on v1

--- a/solution.py
+++ b/solution.py
@@ -1,6 +1,6 @@
+import math
 import jax
 import jax.numpy as jnp
-import numpy as np
 from jax import lax
 from jax.experimental import pallas as pl
 from jax.experimental.pallas import tpu as pltpu
@@ -96,8 +96,9 @@
 
 
 def layer_kernel(
-    span_ref, hidden_ref, gain_ref, inverse_ref, q_gain_ref, k_gain_ref, wq_hbm, wkv_hbm, wo_hbm,
+    span_hbm, hidden_hbm, gain_hbm, q_gain_hbm, k_gain_hbm, wq_hbm, wkv_hbm, wo_hbm,
     out_ref,
+    span_ref, hidden_ref, gain_ref, q_gain_ref, k_gain_ref, wkv_t_ref,
     rows_ref, wq_ref, wkv_ref, wo_ref, cos_ref, sin_ref, query_ref, kv_send, kv_in, key_own, key_other,
     value_other, part_ref, x_in, up_in, down_in, line_out,
     w_sem, row_recv, row_x_send, row_line_send, row_line_send2, kv_ssem, kv_rsem, pair_ssem, pair_rsem,
@@ -107,7 +108,7 @@
     s = lax.axis_index("seq")
     z = t // X
     x = t % X
-    block = hidden_ref.shape[0]
+    block = hidden_hbm.shape[1]
     chunk = X * block
     span_len = Z * chunk
     x_peer = z * X + (1 - x)
@@ -116,14 +117,20 @@
     near = [far, 5 - far, 1, 0]
     order = [low * v + (1 - low) * (3 - v) for v in near]
 
+    small_copies = [
+        pltpu.make_async_copy(source, target, w_sem.at[3 + i])
+        for i, (source, target) in enumerate([
+            (hidden_hbm.at[0], hidden_ref), (gain_hbm, gain_ref), (span_hbm, span_ref),
+            (q_gain_hbm, q_gain_ref), (k_gain_hbm, k_gain_ref),
+        ])
+    ]
+    for copy in small_copies:
+        copy.start()
     weight_copies = [
         pltpu.make_async_copy(wq_hbm, wq_ref, w_sem.at[0]),
         pltpu.make_async_copy(wkv_hbm, wkv_ref, w_sem.at[1]),
         pltpu.make_async_copy(wo_hbm, wo_ref, w_sem.at[2]),
     ]
-    for copy in weight_copies:
-        copy.start()
-
     barrier = pltpu.get_barrier_semaphore()
     for step in range(1, Z * X):
         pl.semaphore_signal(
@@ -131,10 +138,12 @@
         )
     pl.semaphore_signal(barrier, inc=1, device_id={"seq": 1 - s}, device_id_type=MESH)
 
+    small_copies[0].wait()
+    small_copies[1].wait()
     own = hidden_ref[...].astype(jnp.float32)
     scale = lax.rsqrt(jnp.mean(own * own, axis=-1, keepdims=True) + epsilon)
     own_start = pl.multiple_of(t * block, block)
-    rows_ref[pl.ds(own_start, block), :] = (own * scale * gain_ref[...]).astype(jnp.bfloat16)
+    rows_ref[pl.ds(own_start, block), :] = (own * scale * gain_ref[...][None]).astype(jnp.bfloat16)
     pl.semaphore_wait(barrier, Z * X)
 
     def row_copy(zb, xb, target, send_sem):
@@ -169,8 +178,12 @@
         across(zb).start()
 
     forward(z)
-
-    inverse = inverse_ref[...]
+    for copy in weight_copies:
+        copy.start()
+    for copy in small_copies[2:]:
+        copy.wait()
+    power = lax.broadcasted_iota(jnp.int32, (1, HD), 1) % (HD // 2)
+    inverse = jnp.exp(power.astype(jnp.float32) * (-math.log(1000000.0) / (HD // 2)))
     position = span_ref[s] * span_len + lax.broadcasted_iota(jnp.int32, (span_len, HD), 0)
     angles = position.astype(jnp.float32) * inverse
     cos_ref[...] = jnp.cos(angles)
@@ -198,9 +211,7 @@
     def project(zb):
         place = pl.ds(pl.multiple_of(zb * chunk, chunk), chunk)
         rows = rows_ref[place, :]
-        kv = lax.dot_general(
-            rows, wkv_ref[...], (((1,), (1,)), ((), ())), preferred_element_type=jnp.float32
-        ).astype(jnp.bfloat16)
+        kv = jnp.dot(rows, wkv_t_ref[...], preferred_element_type=jnp.float32).astype(jnp.bfloat16)
         for j in range(2):
             kv_send[zb, j] = kv[:, j * HD : (j + 1) * HD]
             here = (2 * t + j) % (Z * X) == t
@@ -215,10 +226,11 @@
 
         raw = jnp.dot(rows, wq_ref[...], preferred_element_type=jnp.float32)
         for j in range(2):
-            q = norm_rotate(raw[:, j * HD : (j + 1) * HD], q_gain_ref[...], zb) * HD ** (-0.5)
+            q = norm_rotate(raw[:, j * HD : (j + 1) * HD], q_gain_ref[...][None], zb) * HD ** (-0.5)
             query_ref[zb, j * chunk : (j + 1) * chunk, :] = q.astype(jnp.bfloat16)
 
     weight_copies[1].wait()
+    wkv_t_ref[...] = wkv_ref[...].T
     weight_copies[0].wait()
     for k in range(1, Z):
         zb = order[k]
@@ -257,7 +269,7 @@
         kv_arrived(0, zb)
         place = slice(zb * chunk, (zb + 1) * chunk)
         raw = kv_in[0, place, :].astype(jnp.float32)
-        key_own[place, :] = norm_rotate(raw, k_gain_ref[...], zb).astype(jnp.bfloat16)
+        key_own[place, :] = norm_rotate(raw, k_gain_ref[...][None], zb).astype(jnp.bfloat16)
         pair_copy(0, zb, key_own, key_other).start()
         kv_arrived(1, zb)
         pair_copy(1, zb, values, value_other).start()
@@ -406,18 +418,22 @@
     _, block, width = hidden_in.shape
     chunk = X * block
     span_len = Z * chunk
-    inverse = 1000000.0 ** (-2.0 * np.arange(HD // 2) / HD)
-    inverse = jnp.asarray(np.concatenate([inverse, inverse])[None], jnp.float32)
     vmem = pl.BlockSpec(memory_space=pltpu.VMEM)
-    anywhere = pl.BlockSpec(memory_space=pl.ANY)
+    hbm = pl.BlockSpec(memory_space=pltpu.HBM)
     bf16 = jnp.bfloat16
     dma = pltpu.SemaphoreType.DMA
     out = pl.pallas_call(
         layer_kernel,
         out_shape=jax.ShapeDtypeStruct((block, width), bf16),
-        in_specs=[pl.BlockSpec(memory_space=pltpu.SMEM)] + [vmem] * 5 + [anywhere] * 3,
+        in_specs=[hbm] * 8,
         out_specs=vmem,
         scratch_shapes=[
+            pltpu.SMEM(span_order.shape, jnp.int32),
+            pltpu.VMEM((block, width), bf16),
+            pltpu.VMEM(norm_gain.shape, jnp.float32),
+            pltpu.VMEM(q_gain.shape, jnp.float32),
+            pltpu.VMEM(k_gain.shape, jnp.float32),
+            pltpu.VMEM((width, w_keyval_t.shape[0]), bf16),
             pltpu.VMEM((span_len, width), bf16),
             pltpu.VMEM(w_query.shape, bf16),
             pltpu.VMEM(w_keyval_t.shape, bf16),
@@ -435,7 +451,7 @@
             pltpu.VMEM((Z, block, width), bf16),
             pltpu.VMEM((Z, block, width), bf16),
             pltpu.VMEM((Z, block, width), bf16),
-            dma((3,)),
+            dma((8,)),
             dma((Z * X,)),
             dma((Z,)),
             dma((Z,)),
@@ -454,7 +470,7 @@
             collective_id=0, has_side_effects=True, vmem_limit_bytes=48 * 1024 * 1024
         ),
     )(
-        span_order, hidden_in[0], norm_gain[None], inverse, q_gain[None], k_gain[None],
+        span_order, hidden_in, norm_gain, q_gain, k_gain,
         w_query, w_keyval_t, w_out,
     )
     return out[None]

time: 93 us -> 90.7 us (0.975)
  Pallas kernels: 83.7 us -> 82.1 us
    pallas_call x1, Pallas kernels: 83.7 us -> 82.1 us  [fused_body(): pl.pallas_call(layer_kernel, out_shape=jax.ShapeDtypeStruct((block, width...]
where the time goes in v2:
time: 90.7 us; the launch traced here: 90.4 us
  Pallas kernels  82.1 us (91%)
  local copies, waits for them, and re-layouts  8.32 us (9%)
    pallas_call x1, Pallas kernels, fused_body(): pl.pallas_call(layer_kernel, out_shape=jax.ShapeDtypeStruct((block, width...  82.1 us
    unnamed x17, local copies, waits for them, and re-layouts  8.32 us

profile of v2, /device:TPU:0, one launch (start us, length us, event | category | flops | bytes accessed | tf_op | source)
XLA Modules:
  0.0 90.4 jit_solution(17446847717228588153)
XLA Ops:
  0.0 0.0 copy-start
  0.0 1.3 %copy-done = bf16[2560,256]{1,0:T(8,128)(2,1)S(1)} copy-done((bf16[2560,256]{1,0:T(8,128)(2,1)S(1)}, bf16[2560,256]{1,0:T(8,128)(2,1)}, u32[]{:S(2)}) %copy-start) | copy-done | bytes 1310744
  1.3 0.0 copy-start.1
  1.3 1.3 %copy-done.1 = bf16[256,2560]{1,0:T(8,128)(2,1)S(1)} copy-done((bf16[256,2560]{1,0:T(8,128)(2,1)S(1)}, bf16[256,2560]{1,0:T(8,128)(2,1)}, u32[]{:S(2)}) %copy-start.1) | copy-done | bytes 1310744
  2.6 0.0 copy-start.2
  2.6 1.3 %copy-done.2 = bf16[256,2560]{1,0:T(8,128)(2,1)S(1)} copy-done((bf16[256,2560]{1,0:T(8,128)(2,1)S(1)}, bf16[256,2560]{1,0:T(8,128)(2,1)}, u32[]{:S(2)}) %copy-start.2) | copy-done | bytes 1310744
  4.0 0.0 copy-start.3
  4.0 1.0 %copy-done.3 = bf16[1,64,2560]{2,1,0:T(8,128)(2,1)S(1)} copy-done((bf16[1,64,2560]{2,1,0:T(8,128)(2,1)S(1)}, bf16[1,64,2560]{2,1,0:T(8,128)(2,1)}, u32[]{:S(2)}) %copy-start.3) | copy-done | bytes 327704
  4.9 0.0 copy-start.4
  4.9 0.7 copy-done.4
  5.6 0.0 copy-start.5
  5.6 0.7 copy-done.5
  6.3 0.0 copy-start.6
  6.3 0.7 copy-done.6
  6.9 0.0 copy-start.7
  6.9 0.7 copy-done.7
  7.6 82.1 %shard_map.82 = bf16[64,2560]{1,0:T(8,128)(2,1)S(1)} custom-call(s32[2]{0:T(128)S(1)} %copy-done.5, bf16[1,64,2560]{2,1,0:T(8,128)(2,1)S(1)} %copy-done.3, f32[2560]{0:T(1024)S(1)} %copy-done.4, f32[128]{0:T(128)S(1)} %copy-done.6, f32[128]{0:T(128)S(1)} %copy-done.7, bf16[2560,256]{1,0:T(8,128)(2,1)S(1)} %copy-done, bf16[256,2560]{1,0:T(8,128)(2,1)S(1)} %copy-done.1, ...), custom_call_target="tpu_custom_call" | custom-call | tf_op jit(solution)/shard_map/pallas_call | solution.py:425
  89.7 0.7 copy.10
Async XLA Ops:
  0.0 1.3 %copy-start = (bf16[2560,256]{1,0:T(8,128)(2,1)S(1)}, bf16[2560,256]{1,0:T(8,128)(2,1)}, u32[]{:S(2)}) copy-start(bf16[2560,256]{1,0:T(8,128)(2,1)} %wq_hbm.1) | copy-start | bytes 3932164
  1.3 1.3 %copy-start.1 = (bf16[256,2560]{1,0:T(8,128)(2,1)S(1)}, bf16[256,2560]{1,0:T(8,128)(2,1)}, u32[]{:S(2)}) copy-start(bf16[256,2560]{1,0:T(8,128)(2,1)} %wkv_hbm.1) | copy-start | bytes 3932164
  2.6 1.3 %copy-start.2 = (bf16[256,2560]{1,0:T(8,128)(2,1)S(1)}, bf16[256,2560]{1,0:T(8,128)(2,1)}, u32[]{:S(2)}) copy-start(bf16[256,2560]{1,0:T(8,128)(2,1)} %wo_hbm.1) | copy-start | bytes 3932164
  4.0 1.0 %copy-start.3 = (bf16[1,64,2560]{2,1,0:T(8,128)(2,1)S(1)}, bf16[1,64,2560]{2,1,0:T(8,128)(2,1)}, u32[]{:S(2)}) copy-start(bf16[1,64,2560]{2,1,0:T(8,128)(2,1)} %hidden_hbm.1) | copy-start | bytes 983044
  4.9 0.7 copy-start.4
  5.6 0.7 copy-start.5
  6.3 0.7 copy-start.6
  6.9 0.7 copy-start.7

commit v3 on v2

--- a/solution.py
+++ b/solution.py
@@ -109,6 +109,7 @@
     z = t // X
     x = t % X
     block = hidden_hbm.shape[1]
+    half = block // 2
     chunk = X * block
     span_len = Z * chunk
     x_peer = z * X + (1 - x)
@@ -146,38 +147,39 @@
     rows_ref[pl.ds(own_start, block), :] = (own * scale * gain_ref[...][None]).astype(jnp.bfloat16)
     pl.semaphore_wait(barrier, Z * X)
 
-    def row_copy(zb, xb, target, send_sem):
-        place = pl.ds(pl.multiple_of((zb * X + xb) * block, block), block)
+    def row_copy(zb, xb, h, target, send_sem):
+        place = pl.ds(pl.multiple_of((zb * X + xb) * block + h * half, half), half)
         return pltpu.make_async_remote_copy(
             src_ref=rows_ref.at[place, :],
             dst_ref=rows_ref.at[place, :],
-            send_sem=send_sem.at[zb],
-            recv_sem=row_recv.at[zb * X + xb],
+            send_sem=send_sem.at[zb, h],
+            recv_sem=row_recv.at[zb * X + xb, h],
             device_id={"tensor": target},
             device_id_type=MESH,
         )
 
-    def line_up(zb):
-        return row_copy(zb, x, (t + X) % (Z * X), row_line_send)
-
-    def line_down(zb):
-        return row_copy(zb, x, (t + Z * X - X) % (Z * X), row_line_send2)
-
-    def across(zb):
-        return row_copy(zb, x, x_peer, row_x_send)
-
-    def forward(zb):
+    def line_up(zb, h):
+        return row_copy(zb, x, h, (t + X) % (Z * X), row_line_send)
+
+    def line_down(zb, h):
+        return row_copy(zb, x, h, (t + Z * X - X) % (Z * X), row_line_send2)
+
+    def across(zb, h):
+        return row_copy(zb, x, h, x_peer, row_x_send)
+
+    def forward(zb, h):
         @pl.when((zb <= z) & (z < Z - 1))
         def _():
-            line_up(zb).start()
+            line_up(zb, h).start()
 
         @pl.when((zb >= z) & (z > 0))
         def _():
-            line_down(zb).start()
-
-        across(zb).start()
-
-    forward(z)
+            line_down(zb, h).start()
+
+        across(zb, h).start()
+
+    for h in range(2):
+        forward(z, h)
     for copy in weight_copies:
         copy.start()
     for copy in small_copies[2:]:
@@ -233,12 +235,15 @@
     wkv_t_ref[...] = wkv_ref[...].T
     weight_copies[0].wait()
     for k in range(1, Z):
-        zb = order[k]
-        row_copy(zb, x, x_peer, row_x_send).wait_recv()
-        forward(zb)
-        row_copy(order[k - 1], 1 - x, x_peer, row_x_send).wait_recv()
-        project(order[k - 1])
-    row_copy(order[Z - 1], 1 - x, x_peer, row_x_send).wait_recv()
+        for h in range(2):
+            row_copy(order[k], x, h, x_peer, row_x_send).wait_recv()
+            forward(order[k], h)
+        for done in ([], [0], [1, 2])[k - 1]:
+            for h in range(2):
+                row_copy(order[done], 1 - x, h, x_peer, row_x_send).wait_recv()
+            project(order[done])
+    for h in range(2):
+        row_copy(order[Z - 1], 1 - x, h, x_peer, row_x_send).wait_recv()
     project(order[Z - 1])
 
     def pair_copy(index, zb, source, target):
@@ -306,108 +311,125 @@
             jnp.bfloat16
         )
 
-    def part_copy(zb):
-        place = pl.ds(pl.multiple_of((1 - x) * block, block), block)
+    def part_copy(zb, h):
+        place = pl.ds(pl.multiple_of((1 - x) * block + h * half, half), half)
         return pltpu.make_async_remote_copy(
             src_ref=part_ref.at[zb, place, :],
-            dst_ref=x_in.at[zb],
-            send_sem=x_ssem.at[zb],
-            recv_sem=x_rsem.at[zb],
+            dst_ref=x_in.at[zb, pl.ds(h * half, half), :],
+            send_sem=x_ssem.at[zb, h],
+            recv_sem=x_rsem.at[zb, h],
             device_id={"tensor": x_peer},
             device_id_type=MESH,
         )
 
-    def sum_up(zb):
+    def sum_copy(zb, h, target_ref, recv_sem, target):
+        place = pl.ds(h * half, half)
         return pltpu.make_async_remote_copy(
-            src_ref=line_out.at[zb], dst_ref=up_in.at[zb], send_sem=line_ssem.at[zb],
-            recv_sem=up_rsem.at[zb], device_id={"tensor": (t + X) % (Z * X)}, device_id_type=MESH,
-        )
-
-    def sum_down(zb):
-        return pltpu.make_async_remote_copy(
-            src_ref=line_out.at[zb], dst_ref=down_in.at[zb], send_sem=line_ssem.at[zb],
-            recv_sem=down_rsem.at[zb], device_id={"tensor": (t + Z * X - X) % (Z * X)},
+            src_ref=line_out.at[zb, place, :],
+            dst_ref=target_ref.at[zb, place, :],
+            send_sem=line_ssem.at[zb, h],
+            recv_sem=recv_sem.at[zb, h],
+            device_id={"tensor": target},
             device_id_type=MESH,
         )
+
+    def sum_up(zb, h):
+        return sum_copy(zb, h, up_in, up_rsem, (t + X) % (Z * X))
+
+    def sum_down(zb, h):
+        return sum_copy(zb, h, down_in, down_rsem, (t + Z * X - X) % (Z * X))
 
     back = order[::-1]
     for zb in back:
         attend(zb)
-        part_copy(zb).start()
-
-    own_half = pl.ds(pl.multiple_of(x * block, block), block)
-
-    def pair_sum(zb):
-        return part_ref[zb, own_half, :].astype(jnp.float32) + x_in[zb].astype(jnp.float32)
+        for h in range(2):
+            part_copy(zb, h).start()
+
+    def pair_sum(zb, h):
+        own_half = pl.ds(pl.multiple_of(x * block + h * half, half), half)
+        mine = part_ref[zb, own_half, :].astype(jnp.float32)
+        return mine + x_in[zb, h * half : (h + 1) * half, :].astype(jnp.float32)
+
+    def combine(zb, h):
+        place = slice(h * half, (h + 1) * half)
+        part_copy(zb, h).wait_recv()
+
+        @pl.when(zb > z)
+        def _():
+            @pl.when(z > 0)
+            def _():
+                sum_up(zb, h).wait_recv()
+                line_out[zb, place, :] = (
+                    pair_sum(zb, h) + up_in[zb, place, :].astype(jnp.float32)
+                ).astype(jnp.bfloat16)
+
+            @pl.when(z == 0)
+            def _():
+                line_out[zb, place, :] = pair_sum(zb, h).astype(jnp.bfloat16)
+
+            sum_up(zb, h).start()
+
+        @pl.when(zb < z)
+        def _():
+            @pl.when(z < Z - 1)
+            def _():
+                sum_down(zb, h).wait_recv()
+                line_out[zb, place, :] = (
+                    pair_sum(zb, h) + down_in[zb, place, :].astype(jnp.float32)
+                ).astype(jnp.bfloat16)
+
+            @pl.when(z == Z - 1)
+            def _():
+                line_out[zb, place, :] = pair_sum(zb, h).astype(jnp.bfloat16)
+
+            sum_down(zb, h).start()
 
     for zb in back[: Z - 1]:
-        part_copy(zb).wait_recv()
-
-        @pl.when(zb > z)
-        def _():
-            @pl.when(z > 0)
-            def _():
-                sum_up(zb).wait_recv()
-                line_out[zb] = (pair_sum(zb) + up_in[zb].astype(jnp.float32)).astype(jnp.bfloat16)
-
-            @pl.when(z == 0)
-            def _():
-                line_out[zb] = pair_sum(zb).astype(jnp.bfloat16)
-
-            sum_up(zb).start()
-
-        @pl.when(zb < z)
-        def _():
-            @pl.when(z < Z - 1)
-            def _():
-                sum_down(zb).wait_recv()
-                line_out[zb] = (pair_sum(zb) + down_in[zb].astype(jnp.float32)).astype(jnp.bfloat16)
-
-            @pl.when(z == Z - 1)
-            def _():
-                line_out[zb] = pair_sum(zb).astype(jnp.bfloat16)
-
-            sum_down(zb).start()
-
-    part_copy(z).wait_recv()
-    total = hidden_ref[...].astype(jnp.float32) + pair_sum(z)
-
-    @pl.when(z == 0)
-    def _():
-        sum_down(z).wait_recv()
-        out_ref[...] = (total + down_in[z].astype(jnp.float32)).astype(jnp.bfloat16)
-
-    @pl.when(z == Z - 1)
-    def _():
-        sum_up(z).wait_recv()
-        out_ref[...] = (total + up_in[z].astype(jnp.float32)).astype(jnp.bfloat16)
-
-    @pl.when((z > 0) & (z < Z - 1))
-    def _():
-        sum_down(z).wait_recv()
-        sum_up(z).wait_recv()
-        out_ref[...] = (
-            total + down_in[z].astype(jnp.float32) + up_in[z].astype(jnp.float32)
-        ).astype(jnp.bfloat16)
+        for h in range(2):
+            combine(zb, h)
+
+    for h in range(2):
+        place = slice(h * half, (h + 1) * half)
+        part_copy(z, h).wait_recv()
+        total = hidden_ref[place, :].astype(jnp.float32) + pair_sum(z, h)
+
+        @pl.when(z == 0)
+        def _():
+            sum_down(z, h).wait_recv()
+            out_ref[place, :] = (total + down_in[z, place, :].astype(jnp.float32)).astype(jnp.bfloat16)
+
+        @pl.when(z == Z - 1)
+        def _():
+            sum_up(z, h).wait_recv()
+            out_ref[place, :] = (total + up_in[z, place, :].astype(jnp.float32)).astype(jnp.bfloat16)
+
+        @pl.when((z > 0) & (z < Z - 1))
+        def _():
+            sum_down(z, h).wait_recv()
+            sum_up(z, h).wait_recv()
+            out_ref[place, :] = (
+                total + down_in[z, place, :].astype(jnp.float32) + up_in[z, place, :].astype(jnp.float32)
+            ).astype(jnp.bfloat16)
 
     for zb in range(Z):
-        across(zb).wait_send()
-        part_copy(zb).wait_send()
+        for h in range(2):
+            across(zb, h).wait_send()
+            part_copy(zb, h).wait_send()
+
+            @pl.when((zb <= z) & (z < Z - 1))
+            def _():
+                line_up(zb, h).wait_send()
+
+            @pl.when((zb >= z) & (z > 0))
+            def _():
+                line_down(zb, h).wait_send()
+
+            @pl.when(zb != z)
+            def _():
+                sum_up(zb, h).wait_send()
+
         pair_copy(0, zb, key_own, key_other).wait_send()
         pair_copy(1, zb, values, value_other).wait_send()
-
-        @pl.when((zb <= z) & (z < Z - 1))
-        def _():
-            line_up(zb).wait_send()
-
-        @pl.when((zb >= z) & (z > 0))
-        def _():
-            line_down(zb).wait_send()
-
-        @pl.when(zb != z)
-        def _():
-            sum_up(zb).wait_send()
-
         for j in range(2):
             @pl.when((2 * t + j) % (Z * X) != t)
             def _():
@@ -452,22 +474,22 @@
             pltpu.VMEM((Z, block, width), bf16),
             pltpu.VMEM((Z, block, width), bf16),
             dma((8,)),
-            dma((Z * X,)),
-            dma((Z,)),
-            dma((Z,)),
-            dma((Z,)),
+            dma((Z * X, 2)),
+            dma((Z, 2)),
+            dma((Z, 2)),
+            dma((Z, 2)),
             dma((Z, 2)),
             dma((2, Z)),
             dma((2, Z)),
             dma((2, Z)),
-            dma((Z,)),
-            dma((Z,)),
-            dma((Z,)),
-            dma((Z,)),
-            dma((Z,)),
+            dma((Z, 2)),
+            dma((Z, 2)),
+            dma((Z, 2)),
+            dma((Z, 2)),
+            dma((Z, 2)),
         ],
         compiler_params=pltpu.CompilerParams(
-            collective_id=0, has_side_effects=True, vmem_limit_bytes=48 * 1024 * 1024
+            collective_id=0, has_side_effects=True, vmem_limit_bytes=64 * 1024 * 1024
         ),
     )(
         span_order, hidden_in, norm_gain, q_gain, k_gain,
@@ -492,7 +514,7 @@
             mesh.shape["tensor"] == Z * X
             and mesh.shape["seq"] == 2
             and w_query.shape[1] == 2 * HD
-            and hidden_in.shape[1] % 16 == 0
+            and hidden_in.shape[1] % 32 == 0
         )
         run = fused_body if fits else body
         return run(hidden_in, span_order, norm_gain, w_query, *rest)

time: 90.7 us -> 78.6 us (0.87)
  local copies, waits for them, and re-layouts: 8.32 us -> 1.72 us
  Pallas kernels: 82.1 us -> 76.7 us
    unnamed x17 -> x1, local copies, waits for them, and re-layouts: 8.32 us -> 1.72 us
    pallas_call x1, Pallas kernels: 82.1 us -> 76.7 us  [fused_body(): pl.pallas_call(layer_kernel, out_shape=jax.ShapeDtypeStruct((block, width...]
where the time goes in v3:
time: 78.6 us; the launch traced here: 78.4 us
  Pallas kernels  76.7 us (98%)
  local copies, waits for them, and re-layouts  1.72 us (2%)
    pallas_call x1, Pallas kernels, fused_body(): pl.pallas_call(layer_kernel, out_shape=jax.ShapeDtypeStruct((block, width...  76.7 us
    unnamed x1, local copies, waits for them, and re-layouts  1.72 us

profile of v3, /device:TPU:0, one launch (start us, length us, event | category | flops | bytes accessed | tf_op | source)
XLA Modules:
  0.0 78.4 jit_solution(16868025734274667675)
XLA Ops:
  0.0 76.7 %shard_map.82 = bf16[64,2560]{1,0:T(8,128)(2,1)} custom-call(s32[2]{0:T(128)} %span_hbm.1, bf16[1,64,2560]{2,1,0:T(8,128)(2,1)} %hidden_hbm.1, f32[2560]{0:T(1024)} %gain_hbm.1, f32[128]{0:T(128)} %q_gain_hbm.1, f32[128]{0:T(128)} %k_gain_hbm.1, bf16[2560,256]{1,0:T(8,128)(2,1)} %wq_hbm.1, bf16[256,2560]{1,0:T(8,128)(2,1)} %wkv_hbm.1, bf16[256,2560]{1,0:T(8,128)(2,1)} %wo_hbm.1), custom_call_target="tpu_custom_call" | custom-call | tf_op jit(solution)/shard_map/pallas_call | solution.py:447
  76.7 1.7 %copy.10 = bf16[1,64,2560]{2,1,0:T(8,128)(2,1)} copy(bf16[1,64,2560]{2,1,0:T(8,128)(2,1)} %bitcast.1) | data formatting | bytes 655360

commit v4 on v3

--- a/solution.py
+++ b/solution.py
@@ -93,6 +93,7 @@
 MESH = pl.DeviceIdType.MESH
 Z = 4
 X = 2
+PIECES = 4
 
 
 def layer_kernel(
@@ -109,7 +110,7 @@
     z = t // X
     x = t % X
     block = hidden_hbm.shape[1]
-    half = block // 2
+    piece = block // PIECES
     chunk = X * block
     span_len = Z * chunk
     x_peer = z * X + (1 - x)
@@ -148,7 +149,7 @@
     pl.semaphore_wait(barrier, Z * X)
 
     def row_copy(zb, xb, h, target, send_sem):
-        place = pl.ds(pl.multiple_of((zb * X + xb) * block + h * half, half), half)
+        place = pl.ds(pl.multiple_of((zb * X + xb) * block + h * piece, piece), piece)
         return pltpu.make_async_remote_copy(
             src_ref=rows_ref.at[place, :],
             dst_ref=rows_ref.at[place, :],
@@ -178,7 +179,7 @@
 
         across(zb, h).start()
 
-    for h in range(2):
+    for h in range(PIECES):
         forward(z, h)
     for copy in weight_copies:
         copy.start()
@@ -235,14 +236,14 @@
     wkv_t_ref[...] = wkv_ref[...].T
     weight_copies[0].wait()
     for k in range(1, Z):
-        for h in range(2):
+        for h in range(PIECES):
             row_copy(order[k], x, h, x_peer, row_x_send).wait_recv()
             forward(order[k], h)
         for done in ([], [0], [1, 2])[k - 1]:
-            for h in range(2):
+            for h in range(PIECES):
                 row_copy(order[done], 1 - x, h, x_peer, row_x_send).wait_recv()
             project(order[done])
-    for h in range(2):
+    for h in range(PIECES):
         row_copy(order[Z - 1], 1 - x, h, x_peer, row_x_send).wait_recv()
     project(order[Z - 1])
 
@@ -312,10 +313,10 @@
         )
 
     def part_copy(zb, h):
-        place = pl.ds(pl.multiple_of((1 - x) * block + h * half, half), half)
+        place = pl.ds(pl.multiple_of((1 - x) * block + h * piece, piece), piece)
         return pltpu.make_async_remote_copy(
             src_ref=part_ref.at[zb, place, :],
-            dst_ref=x_in.at[zb, pl.ds(h * half, half), :],
+            dst_ref=x_in.at[zb, pl.ds(h * piece, piece), :],
             send_sem=x_ssem.at[zb, h],
             recv_sem=x_rsem.at[zb, h],
             device_id={"tensor": x_peer},
@@ -323,7 +324,7 @@
         )
 
     def sum_copy(zb, h, target_ref, recv_sem, target):
-        place = pl.ds(h * half, half)
+        place = pl.ds(h * piece, piece)
         return pltpu.make_async_remote_copy(
             src_ref=line_out.at[zb, place, :],
             dst_ref=target_ref.at[zb, place, :],
@@ -342,16 +343,16 @@
     back = order[::-1]
     for zb in back:
         attend(zb)
-        for h in range(2):
+        for h in range(PIECES):
             part_copy(zb, h).start()
 
     def pair_sum(zb, h):
-        own_half = pl.ds(pl.multiple_of(x * block + h * half, half), half)
+        own_half = pl.ds(pl.multiple_of(x * block + h * piece, piece), piece)
         mine = part_ref[zb, own_half, :].astype(jnp.float32)
-        return mine + x_in[zb, h * half : (h + 1) * half, :].astype(jnp.float32)
+        return mine + x_in[zb, h * piece : (h + 1) * piece, :].astype(jnp.float32)
 
     def combine(zb, h):
-        place = slice(h * half, (h + 1) * half)
+        place = slice(h * piece, (h + 1) * piece)
         part_copy(zb, h).wait_recv()
 
         @pl.when(zb > z)
@@ -385,11 +386,11 @@
             sum_down(zb, h).start()
 
     for zb in back[: Z - 1]:
-        for h in range(2):
+        for h in range(PIECES):
             combine(zb, h)
 
-    for h in range(2):
-        place = slice(h * half, (h + 1) * half)
+    for h in range(PIECES):
+        place = slice(h * piece, (h + 1) * piece)
         part_copy(z, h).wait_recv()
         total = hidden_ref[place, :].astype(jnp.float32) + pair_sum(z, h)
 
@@ -412,7 +413,7 @@
             ).astype(jnp.bfloat16)
 
     for zb in range(Z):
-        for h in range(2):
+        for h in range(PIECES):
             across(zb, h).wait_send()
             part_copy(zb, h).wait_send()
 
@@ -474,19 +475,19 @@
             pltpu.VMEM((Z, block, width), bf16),
             pltpu.VMEM((Z, block, width), bf16),
             dma((8,)),
-            dma((Z * X, 2)),
-            dma((Z, 2)),
-            dma((Z, 2)),
-            dma((Z, 2)),
-            dma((Z, 2)),
+            dma((Z * X, PIECES)),
+            dma((Z, PIECES)),
+            dma((Z, PIECES)),
+            dma((Z, PIECES)),
+            dma((Z, PIECES)),
             dma((2, Z)),
             dma((2, Z)),
             dma((2, Z)),
-            dma((Z, 2)),
-            dma((Z, 2)),
-            dma((Z, 2)),
-            dma((Z, 2)),
-            dma((Z, 2)),
+            dma((Z, PIECES)),
+            dma((Z, PIECES)),
+            dma((Z, PIECES)),
+            dma((Z, PIECES)),
+            dma((Z, PIECES)),
         ],
         compiler_params=pltpu.CompilerParams(
             collective_id=0, has_side_effects=True, vmem_limit_bytes=64 * 1024 * 1024
@@ -514,7 +515,7 @@
             mesh.shape["tensor"] == Z * X
             and mesh.shape["seq"] == 2
             and w_query.shape[1] == 2 * HD
-            and hidden_in.shape[1] % 32 == 0
+            and hidden_in.shape[1] % (16 * PIECES) == 0
         )
         run = fused_body if fits else body
         return run(hidden_in, span_order, norm_gain, w_query, *rest)

time: 78.6 us -> 78.3 us (level)
  Pallas kernels: 76.7 us -> 75.9 us
    pallas_call x1, Pallas kernels: 76.7 us -> 75.9 us  [fused_body(): pl.pallas_call(layer_kernel, out_shape=jax.ShapeDtypeStruct((block, width...]
where the time goes in v4:
time: 78.3 us; the launch traced here: 77.6 us
  Pallas kernels  75.9 us (97%)
  local copies, waits for them, and re-layouts  1.72 us (2%)
    pallas_call x1, Pallas kernels, fused_body(): pl.pallas_call(layer_kernel, out_shape=jax.ShapeDtypeStruct((block, width...  75.9 us
    unnamed x1, local copies, waits for them, and re-layouts  1.72 us

profile of v4, /device:TPU:0, one launch (start us, length us, event | category | flops | bytes accessed | tf_op | source)
XLA Modules:
  0.0 77.6 jit_solution(15166195026072088851)
XLA Ops:
  0.0 75.9 %shard_map.82 = bf16[64,2560]{1,0:T(8,128)(2,1)} custom-call(s32[2]{0:T(128)} %span_hbm.1, bf16[1,64,2560]{2,1,0:T(8,128)(2,1)} %hidden_hbm.1, f32[2560]{0:T(1024)} %gain_hbm.1, f32[128]{0:T(128)} %q_gain_hbm.1, f32[128]{0:T(128)} %k_gain_hbm.1, bf16[2560,256]{1,0:T(8,128)(2,1)} %wq_hbm.1, bf16[256,2560]{1,0:T(8,128)(2,1)} %wkv_hbm.1, bf16[256,2560]{1,0:T(8,128)(2,1)} %wo_hbm.1), custom_call_target="tpu_custom_call" | custom-call | tf_op jit(solution)/shard_map/pallas_call | solution.py:448
  75.9 1.7 %copy.10 = bf16[1,64,2560]{2,1,0:T(8,128)(2,1)} copy(bf16[1,64,2560]{2,1,0:T(8,128)(2,1)} %bitcast.1) | data formatting | bytes 655360

commit v5 on v4

--- a/solution.py
+++ b/solution.py
@@ -243,10 +243,6 @@
             for h in range(PIECES):
                 row_copy(order[done], 1 - x, h, x_peer, row_x_send).wait_recv()
             project(order[done])
-    for h in range(PIECES):
-        row_copy(order[Z - 1], 1 - x, h, x_peer, row_x_send).wait_recv()
-    project(order[Z - 1])
-
     def pair_copy(index, zb, source, target):
         place = pl.ds(zb * chunk, chunk)
         return pltpu.make_async_remote_copy(
@@ -271,7 +267,7 @@
             ).wait_recv()
 
     values = kv_in.at[1]
-    for zb in range(Z):
+    def share_keys(zb):
         kv_arrived(0, zb)
         place = slice(zb * chunk, (zb + 1) * chunk)
         raw = kv_in[0, place, :].astype(jnp.float32)
@@ -279,6 +275,14 @@
         pair_copy(0, zb, key_own, key_other).start()
         kv_arrived(1, zb)
         pair_copy(1, zb, values, value_other).start()
+
+    for zb in range(1, Z - 1):
+        share_keys(zb)
+    for h in range(PIECES):
+        row_copy(order[Z - 1], 1 - x, h, x_peer, row_x_send).wait_recv()
+    project(order[Z - 1])
+    share_keys(0)
+    share_keys(Z - 1)
     weight_copies[2].wait()
     for zb in range(Z):
         pair_copy(0, zb, key_own, key_other).wait_recv()

time: 78.3 us -> 79.2 us (1.011)
  no operation moved by 1% of the time
where the time goes in v5:
time: 79.2 us; the launch traced here: 78.1 us
  Pallas kernels  76.4 us (96%)
  local copies, waits for them, and re-layouts  1.72 us (2%)
    pallas_call x1, Pallas kernels, fused_body(): pl.pallas_call(layer_kernel, out_shape=jax.ShapeDtypeStruct((block, width...  76.4 us
    unnamed x1, local copies, waits for them, and re-layouts  1.72 us

profile of v5, /device:TPU:0, one launch (start us, length us, event | category | flops | bytes accessed | tf_op | source)
XLA Modules:
  0.0 78.1 jit_solution(3805956298072789758)
XLA Ops:
  0.0 76.4 %shard_map.82 = bf16[64,2560]{1,0:T(8,128)(2,1)} custom-call(s32[2]{0:T(128)} %span_hbm.1, bf16[1,64,2560]{2,1,0:T(8,128)(2,1)} %hidden_hbm.1, f32[2560]{0:T(1024)} %gain_hbm.1, f32[128]{0:T(128)} %q_gain_hbm.1, f32[128]{0:T(128)} %k_gain_hbm.1, bf16[2560,256]{1,0:T(8,128)(2,1)} %wq_hbm.1, bf16[256,2560]{1,0:T(8,128)(2,1)} %wkv_hbm.1, bf16[256,2560]{1,0:T(8,128)(2,1)} %wo_hbm.1), custom_call_target="tpu_custom_call" | custom-call | tf_op jit(solution)/shard_map/pallas_call | solution.py:452
  76.4 1.7 %copy.10 = bf16[1,64,2560]{2,1,0:T(8,128)(2,1)} copy(bf16[1,64,2560]{2,1,0:T(8,128)(2,1)} %bitcast.1) | data formatting | bytes 655360
